TPU v7x, 32 devices: a whole 2x2x4 slice. The times are simulated.
32 devices in a mesh: rep: 8 (over z, core), exp: 4 (over y, x).
Axes of the slice: x: 2, y: 2, z: 4, core: 2. Of those that a mesh axis runs over, the one named last changes fastest.
Arguments:
- tokens: bfloat16 [512, 2048], P('exp'), may hold values from -6 to 6
- expert_ids: int32 [512, 2], P('exp'), may hold values from 0 to 3, all different within a row; in each aligned block of 128 rows (0 to 127, 128 to 255, ...) at most 128 rows name the same one
- gate_values: float32 [512, 2], P('exp'), may hold values from 0.2 to 1
- grad_out: bfloat16 [512, 2048], P('exp'), may hold values from -6 to 6
- w_up: bfloat16 [4, 2048, 8192], P('exp', None, 'rep'), may hold values from -0.125 to 0.125
- w_down: bfloat16 [4, 8192, 2048], P('exp', 'rep'), may hold values from -0.0625 to 0.0625
Outputs:
- mixed: bfloat16 [512, 2048], P('exp', 'rep')
- grad_tokens: bfloat16 [512, 2048], P('exp', 'rep')
- grad_w_up: bfloat16 [4, 2048, 8192], P('exp', None, 'rep')
- grad_w_down: bfloat16 [4, 8192, 2048], P('exp', 'rep')
Inputs may be any that keep to these rules, and one draw needn't show every extreme that they name: `expert_ids`: each row names 2 different experts. Within the rows of one index of exp (aligned blocks of 128 rows) no expert is named by more than 128 rows, a bound that some block reaches.
All inputs are finite; a program needn't handle non-finite values.
Results may differ from a plain program's by a relative error of at most 0.022.
Values may be sent and summed in bfloat16 or wider, within the bound.
A program may use at most 128 MiB of HBM per device.

v0:
```python
import jax
import jax.numpy as jnp
from jax import lax
from jax.sharding import PartitionSpec as P


def plan_slots(routed, experts, capacity):
    flat_ids = routed.reshape(-1)
    onehot = (flat_ids[:, None] == jnp.arange(experts, dtype=jnp.int32)[None, :]).astype(jnp.int32)
    before = jnp.cumsum(onehot, axis=0) - onehot
    position = jnp.sum(before * onehot, axis=1)
    counts = jnp.sum(onehot, axis=0)
    slotting_labels = flat_ids * capacity + position
    placed = (
        slotting_labels[None, :] == jnp.arange(experts * capacity, dtype=jnp.int32)[:, None]
    ).astype(jnp.bfloat16)
    return (placed, counts)


def expert_math(rows_in, rows_grad, live_mask, up_weight, down_weight):
    preact = jnp.dot(rows_in, up_weight, preferred_element_type=jnp.float32)
    sigmoid_val = jax.nn.sigmoid(preact)
    keep = live_mask[:, None]
    hidden_units = jnp.where(keep, preact * sigmoid_val, 0.0).astype(jnp.bfloat16)
    out_part = jnp.dot(hidden_units, down_weight, preferred_element_type=jnp.float32)
    grad_hidden = lax.dot_general(
        rows_grad, down_weight, (((1,), (1,)), ((), ())), preferred_element_type=jnp.float32
    )
    slope = sigmoid_val * (1.0 + preact * (1.0 - sigmoid_val))
    gradient_before_activation = jnp.where(keep, grad_hidden * slope, 0.0).astype(jnp.bfloat16)
    grad_down_e = lax.dot_general(
        hidden_units, rows_grad, (((0,), (0,)), ((), ())), preferred_element_type=jnp.float32
    )
    grad_up_e = lax.dot_general(
        rows_in,
        gradient_before_activation,
        (((0,), (0,)), ((), ())),
        preferred_element_type=jnp.float32,
    )
    dx_part = lax.dot_general(
        gradient_before_activation,
        up_weight,
        (((1,), (1,)), ((), ())),
        preferred_element_type=jnp.float32,
    )
    return (out_part, dx_part, grad_up_e, grad_down_e)


def local(tokens, expert_ids, gate_values, grad_out, w_up, w_down):
    n_rep = lax.axis_size("rep")
    n_exp = lax.axis_size("exp")
    tok_count, width = tokens.shape
    top_k = expert_ids.shape[1]
    pair_count = tok_count * top_k
    capacity = max(2, min(tok_count, 2 * tok_count * top_k // n_exp))
    cols = width // n_rep
    up_weight = w_up[0]
    down_weight = w_down[0]
    grad_rows = (gate_values[:, :, None] * grad_out[:, None, :].astype(jnp.float32)).astype(
        jnp.bfloat16
    )
    grad_rows = grad_rows.reshape(pair_count, width)
    placed, counts = plan_slots(expert_ids, n_exp, capacity)
    summed = placed.reshape(n_exp * capacity, tok_count, top_k).sum(axis=2)
    sent_in = jnp.dot(summed, tokens, preferred_element_type=jnp.float32).astype(jnp.bfloat16)
    sent_grad = jnp.dot(placed, grad_rows, preferred_element_type=jnp.float32).astype(jnp.bfloat16)
    count_parts = jnp.stack([counts // 16, counts % 16], axis=1).astype(jnp.bfloat16)
    got_in, got_grad, got_counts = (
        lax.all_to_all(
            sent_in.reshape(n_exp, capacity, width), "exp", split_axis=0, concat_axis=0, tiled=True
        ),
        lax.all_to_all(
            sent_grad.reshape(n_exp, capacity, width),
            "exp",
            split_axis=0,
            concat_axis=0,
            tiled=True,
        ),
        lax.all_to_all(count_parts, "exp", split_axis=0, concat_axis=0, tiled=True),
    )
    count_values = got_counts[:, 0].astype(jnp.float32) * 16.0 + got_counts[:, 1].astype(
        jnp.float32
    )
    slot_mask = jnp.arange(capacity, dtype=jnp.float32)[None, :] < count_values[:, None]
    rows_in = got_in.reshape(-1, width)
    rows_grad = got_grad.reshape(-1, width)
    live_mask = slot_mask.reshape(-1)
    out_part, dx_part, grad_up_e, grad_down_e = expert_math(
        rows_in, rows_grad, live_mask, up_weight, down_weight
    )
    total_out, total_dx = (
        lax.psum(out_part.astype(jnp.bfloat16), "rep").astype(jnp.float32),
        lax.psum(dx_part.astype(jnp.bfloat16), "rep").astype(jnp.float32),
    )
    col_start = lax.axis_index("rep") * cols
    summed_out = lax.dynamic_slice_in_dim(total_out, col_start, cols, 1)
    summed_dx = lax.dynamic_slice_in_dim(total_dx, col_start, cols, 1)
    back_out, back_dx = (
        lax.all_to_all(
            summed_out.astype(jnp.bfloat16).reshape(n_exp, capacity, cols),
            "exp",
            split_axis=0,
            concat_axis=0,
            tiled=True,
        ),
        lax.all_to_all(
            summed_dx.astype(jnp.bfloat16).reshape(n_exp, capacity, cols),
            "exp",
            split_axis=0,
            concat_axis=0,
            tiled=True,
        ),
    )
    pair_out = jnp.einsum(
        "st,sd->td",
        placed,
        back_out.reshape(n_exp * capacity, cols),
        preferred_element_type=jnp.float32,
    )
    pair_dx = jnp.einsum(
        "st,sd->td",
        placed,
        back_dx.reshape(n_exp * capacity, cols),
        preferred_element_type=jnp.float32,
    )
    mixed = jnp.sum(gate_values[:, :, None] * pair_out.reshape(tok_count, top_k, cols), axis=1)
    grad_tokens = jnp.sum(pair_dx.reshape(tok_count, top_k, cols), axis=1)
    return (
        mixed.astype(jnp.bfloat16),
        grad_tokens.astype(jnp.bfloat16),
        grad_up_e.astype(jnp.bfloat16)[None],
        grad_down_e.astype(jnp.bfloat16)[None],
    )


def solution(mesh):
    return jax.shard_map(
        local,
        mesh=mesh,
        in_specs=(
            P("exp", None),
            P("exp", None),
            P("exp", None),
            P("exp", None),
            P("exp", None, "rep"),
            P("exp", "rep", None),
        ),
        out_specs=(P("exp", "rep"), P("exp", "rep"), P("exp", None, "rep"), P("exp", "rep", None)),
        check_vma=False,
    )
```

profile of v0, /device:TPU:0, one launch (start us, length us, event | category | flops | bytes accessed | tf_op | source)
XLA Modules:
  0.0 217.1 jit_solution(14014729276484896640)
XLA Ops:
  8.3 1.2 reduce-window.6
  10.8 5.2 %all-to-all-start = ((bf16[4,1,2]{2,1,0:T(2,128)(2,1)}), bf16[4,1,2]{2,1,0:T(2,128)(2,1)S(1)}, u32[]{:S(2)}, u32[]{:S(2)}) async-start(bf16[4,1,2]{2,1,0:T(2,128)(2,1)} %copy.47), calls=%async_computation | async-start | bytes 4096 | tf_op jit(solution)/shard_map/all_to_all | solution.py:79
  16.9 2.0 convolution_convert_fusion.1
  18.9 1.6 all-to-all-done
  20.5 4.6 %all-to-all-start.1 = ((bf16[4,128,2048]{2,1,0:T(8,128)(2,1)}), bf16[4,128,2048]{2,1,0:T(8,128)(2,1)}, u32[]{:S(2)}, u32[]{:S(2)}) async-start(bf16[4,128,2048]{2,1,0:T(8,128)(2,1)} %bitcast.9), calls=%async_computation.1 | async-start | bytes 4194304 | tf_op jit(solution)/shard_map/all_to_all | solution.py:69
  25.1 1.0 mul.76
  26.2 2.4 %mul.77 = f32[256,2048]{1,0:T(8,128)} reshape(f32[128,2,2048]{2,1,0:T(2,128)S(1)} %mul.76) | data formatting | bytes 4194304 | tf_op jit(solution)/shard_map/mul | solution.py:59
  28.9 3.7 %convolution_convert_fusion = bf16[512,2048]{1,0:T(8,128)(2,1)} fusion(f32[256,2048]{1,0:T(8,128)} %mul.77, f32[256]{0:T(256)S(1)} %mul.74, s32[256]{0:T(256)S(1)} %multiply_add_fusion), kind=kOutput, calls=%fused_computation.12 | convolution fusion | flops 539099136 | bytes 4196352 | tf_op jit(solution)/shard_map/dot_general | solution.py:66
  32.7 16.2 %all-to-all-done.1 = bf16[4,128,2048]{2,1,0:T(8,128)(2,1)} async-done(((bf16[4,128,2048]{2,1,0:T(8,128)(2,1)}), bf16[4,128,2048]{2,1,0:T(8,128)(2,1)}, u32[]{:S(2)}, u32[]{:S(2)}) %all-to-all-start.1) | async-done | bytes 2097184 | tf_op jit(solution)/shard_map/all_to_all | solution.py:69
  48.9 3.6 %all-to-all-start.3 = ((bf16[4,128,2048]{2,1,0:T(8,128)(2,1)}), bf16[4,128,2048]{2,1,0:T(8,128)(2,1)S(1)}, u32[]{:S(2)}, u32[]{:S(2)}) async-start(bf16[4,128,2048]{2,1,0:T(8,128)(2,1)} %bitcast.16), calls=%async_computation.3 | async-start | bytes 4194304 | tf_op jit(solution)/shard_map/all_to_all | solution.py:72
  52.6 5.3 %fusion.6 = f32[512,1024]{1,0:T(8,128)S(1)} fusion(bf16[512,2048]{1,0:T(8,128)(2,1)} %bitcast.10, bf16[1,2048,1024]{2,1,0:T(8,128)(2,1)} %param.10), kind=kOutput, calls=%fused_computation.6 | convolution fusion | flops 2147483648 | bytes 8388608 | tf_op jit(solution)/shard_map/dot_general | solution.py:21
  57.9 1.3 copy-done.5
  59.2 3.8 %fusion.11 = bf16[512,2048]{1,0:T(8,128)(2,1)} fusion(bf16[1,1024,2048]{2,1,0:T(8,128)(2,1)S(1)} %copy-done.3, f32[512,1024]{1,0:T(8,128)S(1)} %fusion.6, pred[512]{0:T(512)(128)(4,1)S(1)} %fusion.28), kind=kOutput, calls=%fused_computation.11 | convolution fusion | flops 2151677952 | bytes 8389120 | tf_op jit(solution)/shard_map/dot_general | solution.py:25
  63.0 13.8 %all-to-all-done.3 = bf16[4,128,2048]{2,1,0:T(8,128)(2,1)S(1)} async-done(((bf16[4,128,2048]{2,1,0:T(8,128)(2,1)}), bf16[4,128,2048]{2,1,0:T(8,128)(2,1)S(1)}, u32[]{:S(2)}, u32[]{:S(2)}) %all-to-all-start.3) | async-done | bytes 2097184 | tf_op jit(solution)/shard_map/all_to_all | solution.py:72
  76.8 5.8 %select_convert_fusion = bf16[512,1024]{1,0:T(8,128)(2,1)S(1)} fusion(f32[512,1024]{1,0:T(8,128)} %copy-done.5, bf16[512,2048]{1,0:T(8,128)(2,1)S(1)} %bitcast.83, bf16[1,1024,2048]{2,1,0:T(8,128)(2,1)} %param.11, pred[512]{0:T(512)(128)(4,1)S(1)} %fusion.28), kind=kOutput, calls=%fused_computation.14 | convolution fusion | flops 2152726528 | bytes 9437696 | tf_op jit(solution)/shard_map/dot_general | solution.py:26
  82.5 1.1 copy-done.6
  83.6 3.7 %fusion.8 = bf16[512,2048]{1,0:T(8,128)(2,1)} fusion(bf16[512,1024]{1,0:T(8,128)(2,1)S(1)} %select_convert_fusion, bf16[1,2048,1024]{2,1,0:T(8,128)(2,1)S(1)} %copy-done.4), kind=kOutput, calls=%fused_computation.10 | convolution fusion | flops 2148532224 | bytes 7340032 | tf_op jit(solution)/shard_map/dot_general | solution.py:40
  87.4 97.3 %all-reduce.3.cloned.1.call-done = (bf16[512,2048]{1,0:T(8,128)(2,1)}, bf16[512,2048]{1,0:T(8,128)(2,1)}) async-done(((bf16[512,2048]{1,0:T(8,128)(2,1)}, bf16[512,2048]{1,0:T(8,128)(2,1)}), (bf16[512,2048]{1,0:T(8,128)(2,1)}, bf16[512,2048]{1,0:T(8,128)(2,1)})) %all-reduce.3.cloned.1.call-update) | async-done | bytes 4194320 | tf_op jit(solution)/shard_map/psum | solution.py:92
  184.7 1.7 convert_convert_fusion
  186.3 3.8 %all-to-all-start.4 = ((bf16[4,128,256]{2,1,0:T(8,128)(2,1)}), bf16[4,128,256]{2,1,0:T(8,128)(2,1)S(1)}, u32[]{:S(2)}, u32[]{:S(2)}) async-start(bf16[4,128,256]{2,1,0:T(8,128)(2,1)} %bitcast.18), calls=%async_computation.4 | async-start | bytes 524288 | tf_op jit(solution)/shard_map/all_to_all | solution.py:106
  190.2 6.2 %convert_bitcast_fusion = bf16[1,1024,2048]{2,1,0:T(8,128)(2,1)} fusion(bf16[512,2048]{1,0:T(8,128)(2,1)S(1)} %bitcast.84, f32[512,1024]{1,0:T(8,128)} %copy-done.5, pred[512]{0:T(512)(128)(4,1)S(1)} %fusion.28), kind=kOutput, calls=%fused_computation.8 | convolution fusion | flops 2152726528 | bytes 8389120 | tf_op jit(solution)/shard_map/dot_general | solution.py:31
  196.3 1.7 convert_convert_fusion.1
  198.0 4.2 %all-to-all-start.2 = ((bf16[4,128,256]{2,1,0:T(8,128)(2,1)}), bf16[4,128,256]{2,1,0:T(8,128)(2,1)S(1)}, u32[]{:S(2)}, u32[]{:S(2)}) async-start(bf16[4,128,256]{2,1,0:T(8,128)(2,1)} %bitcast.13), calls=%async_computation.2 | async-start | bytes 524288 | tf_op jit(solution)/shard_map/all_to_all | solution.py:99
  202.2 6.2 %convert_bitcast_fusion.1 = bf16[1,2048,1024]{2,1,0:T(8,128)(2,1)} fusion(bf16[512,2048]{1,0:T(8,128)(2,1)} %bitcast.10, bf16[512,1024]{1,0:T(8,128)(2,1)} %copy-done.6), kind=kOutput, calls=%fused_computation.9 | convolution fusion | flops 2149580800 | bytes 7340032 | tf_op jit(solution)/shard_map/dot_general | solution.py:34
  (42 shorter events, 5.7 us)
Async XLA Ops:
  7.2 9.8 %copy-start = (bf16[128,2048]{1,0:T(8,128)(2,1)S(1)}, bf16[128,2048]{1,0:T(8,128)(2,1)}, u32[]{:S(2)}) copy-start(bf16[128,2048]{1,0:T(8,128)(2,1)} %param.6) | copy-start | bytes 1572868
  10.8 9.7 %all-to-all-start = ((bf16[4,1,2]{2,1,0:T(2,128)(2,1)}), bf16[4,1,2]{2,1,0:T(2,128)(2,1)S(1)}, u32[]{:S(2)}, u32[]{:S(2)}) async-start(bf16[4,1,2]{2,1,0:T(2,128)(2,1)} %copy.47), calls=%async_computation | async-start | bytes 4096 | tf_op jit(solution)/shard_map/all_to_all | solution.py:79
  20.5 4.6 %copy-start.1 = (bf16[128,2048]{1,0:T(8,128)(2,1)S(1)}, bf16[128,2048]{1,0:T(8,128)(2,1)}, u32[]{:S(2)}) copy-start(bf16[128,2048]{1,0:T(8,128)(2,1)} %param.9) | copy-start | bytes 1572868
  20.5 28.4 %all-to-all-start.1 = ((bf16[4,128,2048]{2,1,0:T(8,128)(2,1)}), bf16[4,128,2048]{2,1,0:T(8,128)(2,1)}, u32[]{:S(2)}, u32[]{:S(2)}) async-start(bf16[4,128,2048]{2,1,0:T(8,128)(2,1)} %bitcast.9), calls=%async_computation.1 | async-start | bytes 4194304 | tf_op jit(solution)/shard_map/all_to_all | solution.py:69
  26.1 2.5 %copy-start.2 = (f32[128,2]{0,1:T(2,128)S(1)}, f32[128,2]{0,1:T(2,128)}, u32[]{:S(2)}) copy-start(f32[128,2]{0,1:T(2,128)} %param.8) | copy-start | bytes 3076
  48.9 27.9 %all-to-all-start.3 = ((bf16[4,128,2048]{2,1,0:T(8,128)(2,1)}), bf16[4,128,2048]{2,1,0:T(8,128)(2,1)S(1)}, u32[]{:S(2)}, u32[]{:S(2)}) async-start(bf16[4,128,2048]{2,1,0:T(8,128)(2,1)} %bitcast.16), calls=%async_computation.3 | async-start | bytes 4194304 | tf_op jit(solution)/shard_map/all_to_all | solution.py:72
  52.5 132.2 %all-reduce.3.cloned.1.call-start = ((), (), s32[]{:S(2)}) async-start(), calls=%async_computation.5 | async-start | bytes 8388608 | tf_op jit(solution)/shard_map/psum | solution.py:92
  52.6 6.6 %copy-start.3 = (bf16[1,1024,2048]{2,1,0:T(8,128)(2,1)S(1)}, bf16[1,1024,2048]{2,1,0:T(8,128)(2,1)}, u32[]{:S(2)}) copy-start(bf16[1,1024,2048]{2,1,0:T(8,128)(2,1)} %param.11) | copy-start | bytes 12582916
  57.9 1.3 copy-start.5
  76.8 6.8 %copy-start.4 = (bf16[1,2048,1024]{2,1,0:T(8,128)(2,1)S(1)}, bf16[1,2048,1024]{2,1,0:T(8,128)(2,1)}, u32[]{:S(2)}) copy-start(bf16[1,2048,1024]{2,1,0:T(8,128)(2,1)} %param.10) | copy-start | bytes 12582916
  82.5 1.1 copy-start.6
  186.3 11.7 %all-to-all-start.4 = ((bf16[4,128,256]{2,1,0:T(8,128)(2,1)}), bf16[4,128,256]{2,1,0:T(8,128)(2,1)S(1)}, u32[]{:S(2)}, u32[]{:S(2)}) async-start(bf16[4,128,256]{2,1,0:T(8,128)(2,1)} %bitcast.18), calls=%async_computation.4 | async-start | bytes 524288 | tf_op jit(solution)/shard_map/all_to_all | solution.py:106
  198.0 11.4 %all-to-all-start.2 = ((bf16[4,128,256]{2,1,0:T(8,128)(2,1)}), bf16[4,128,256]{2,1,0:T(8,128)(2,1)S(1)}, u32[]{:S(2)}, u32[]{:S(2)}) async-start(bf16[4,128,256]{2,1,0:T(8,128)(2,1)} %bitcast.13), calls=%async_computation.2 | async-start | bytes 524288 | tf_op jit(solution)/shard_map/all_to_all | solution.py:99
Sparse Core Ops, SparseCore 0:
  87.5 97.1 all-reduce.2
where the time goes:
time: 218 us; the launch traced here: 217 us
  waiting for transfers between devices  129 us (59%)
  matrix products  38.5 us (18%)
  starting transfers between devices  21.4 us (10%)
  between operations  14.2 us (7%)
  local copies, waits for them, and re-layouts  8.51 us (4%)
  other arithmetic  5.69 us (3%)
    psum x1, waiting for transfers between devices, local(): lax.psum(out_part.astype(jnp.bfloat16), 'rep').astype(jnp.float32)  97.3 us
    all_to_all x1, waiting for transfers between devices, local(): lax.all_to_all(sent_in.reshape(n_exp, capacity, width), 'exp', split_axis...  16.2 us
    all_to_all x1, waiting for transfers between devices, local(): lax.all_to_all(sent_grad.reshape(n_exp, capacity, width), 'exp', split_ax...  13.8 us
    dot_general x1, matrix products, expert_math(): lax.dot_general(rows_in, gradient_before_activation, (((0,), (0,)), ((),...  6.25 us
    dot_general x1, matrix products, expert_math(): lax.dot_general(hidden_units, rows_grad, (((0,), (0,)), ((), ())), prefer...  6.17 us
    dot_general x1, matrix products, expert_math(): lax.dot_general(rows_grad, down_weight, (((1,), (1,)), ((), ())), preferr...  5.76 us
    dot_general x1, matrix products, expert_math(): preact = jnp.dot(rows_in, up_weight, preferred_element_type=jnp.float32)  5.29 us
    all_to_all x1, starting transfers between devices, local(): lax.all_to_all(count_parts, 'exp', split_axis=0, concat_axis=0, tiled=True)  5.16 us
  transfers between devices with their start and end apart: 6, of which 4 were waited for; matrix products, arithmetic and copies ran while one was open for 16% of the time, Pallas kernels for 0%

commit v1 on v0

--- a/solution.py
+++ b/solution.py
@@ -1,7 +1,319 @@
+import functools
+
 import jax
 import jax.numpy as jnp
 from jax import lax
+from jax.experimental import pallas as pl
+from jax.experimental.pallas import tpu as pltpu
 from jax.sharding import PartitionSpec as P
+
+MESH = pl.DeviceIdType.MESH
+F32 = jnp.float32
+BF16 = jnp.bfloat16
+NN = (((1,), (0,)), ((), ()))
+NT = (((1,), (1,)), ((), ()))
+TN = (((0,), (0,)), ((), ()))
+
+
+def dot(a, b, dims):
+    return lax.dot_general(a, b, dims, preferred_element_type=F32)
+
+
+def fused_kernel(
+    weight_in, tok, gout, up_hbm, down_hbm,
+    mixed_out, gtok_out, gup_hbm, gdown_hbm,
+    x_all, g_all, gr_all, weight_all, coef, up, down, slope, hid, gpre,
+    send_a, recv_a, s_sum, recv_1, mid, recv_2, q_sum, recv_3, gup, gdown,
+    load_sem, meta_send, meta_recv, gat_send, gat_recv,
+    a_send, a_recv, b_send, b_recv, t_send, t_recv, c_send, c_recv, gup_sem, gdown_sem,
+):
+    rep, e = lax.axis_index("rep"), lax.axis_index("exp")
+    z, c = lax.div(rep, 2), lax.rem(rep, 2)
+    y, x = lax.div(e, 2), lax.rem(e, 2)
+    xn, yn = 1 - x, 1 - y
+    ex, ey, ed = y * 2 + xn, yn * 2 + x, yn * 2 + xn
+    p = lax.rem(z, 2)
+    to_x = {"rep": rep, "exp": ex}
+    to_y = {"rep": rep, "exp": ey}
+    to_d = {"rep": rep, "exp": ed}
+    to_sib = {"rep": z * 2 + 1 - c, "exp": e}
+    to_pair = {"rep": (z + 1 - 2 * p) * 2 + c, "exp": e}
+
+    def at_z(d):
+        zz = lax.rem(z + d, 4)
+        return zz, {"rep": zz * 2 + c, "exp": e}
+
+    def remote(src, dst, send, recv, where):
+        return pltpu.make_async_remote_copy(
+            src_ref=src, dst_ref=dst, send_sem=send, recv_sem=recv,
+            device_id=where, device_id_type=MESH,
+        )
+
+    load_up = pltpu.make_async_copy(up_hbm, up, load_sem.at[0])
+    load_down = pltpu.make_async_copy(down_hbm, down, load_sem.at[1])
+    load_up.start()
+    load_down.start()
+
+    barrier = pltpu.get_barrier_semaphore()
+    partners = [to_x, to_y, to_d, to_sib] + [at_z(d)[1] for d in (1, 2, 3)]
+    for who in partners:
+        pl.semaphore_signal(barrier, inc=1, device_id=who, device_id_type=MESH)
+    pl.semaphore_wait(barrier, len(partners))
+
+    lo, own_rows, mid_rows, pair_rows = 64 * c + 16 * p, 64 * c + 48 * p, 64 * c + 16, 64 * c + 48 - 48 * p
+
+    def rows(block, start, count):
+        return pl.ds(pl.multiple_of(block * 128 + start, 16), count)
+
+    class Gather:
+        def __init__(self, t, own, buf):
+            self.t, self.own, self.buf, self.copies = t, own, buf, {}
+
+        def send(self, k, src, block, start, count, where):
+            at = rows(block, start, count)
+            copy = remote(
+                self.buf.at[at] if src is None else src, self.buf.at[at],
+                gat_send.at[self.t, k], gat_recv.at[self.t, k], where,
+            )
+            copy.start()
+            self.copies[k] = copy
+
+        def direct(self):
+            mine = self.own.at[pl.ds(pl.multiple_of(lo, 16), 48)]
+            self.send(0, mine, e, lo, 48, to_x)
+            self.send(1, mine, e, lo, 48, to_y)
+
+        def keep(self):
+            self.buf[rows(e, 0, 128), :] = self.own[...]
+
+        def forward(self):
+            first = (own_rows, 16) if self.t == 0 else (mid_rows, 32)
+            second = (mid_rows, 32) if self.t == 0 else (own_rows, 16)
+            self.copies[0].wait_recv()
+            self.send(2, None, ex, *first, to_y)
+            self.send(4, None, ex, own_rows, 16, to_pair)
+            self.send(7, None, ex, lo, 48, to_sib)
+            self.copies[1].wait_recv()
+            self.send(3, None, ey, *second, to_x)
+            self.send(5, None, ey, own_rows, 16, to_pair)
+            self.send(8, None, ey, lo, 48, to_sib)
+
+        def diagonal(self):
+            self.copies[2].wait_recv()
+            self.copies[3].wait_recv()
+            self.send(6, None, ed, own_rows, 16, to_pair)
+            self.send(9, None, ed, lo, 48, to_sib)
+
+        def pair(self):
+            for k, block in ((4, ex), (5, ey), (6, ed)):
+                self.copies[k].wait_recv()
+                self.send(6 + k, None, block, pair_rows, 16, to_sib)
+
+        def finish(self):
+            for k in range(7, 13):
+                self.copies[k].wait_recv()
+
+        def drain(self):
+            for k in range(13):
+                self.copies[k].wait_send()
+
+    gx, gg = Gather(0, tok, x_all), Gather(1, gout, g_all)
+    gx.direct()
+    weights = []
+    for k, where in enumerate((to_x, to_y, to_d)):
+        copy = remote(weight_in, weight_all.at[e], meta_send.at[k], meta_recv.at[k], where)
+        copy.start()
+        weights.append(copy)
+    gx.keep()
+    gg.keep()
+    weight_all[pl.ds(e, 1)] = weight_in[...][None]
+    for copy in weights:
+        copy.wait_recv()
+    for block in range(4):
+        line = weight_all[block, pl.ds(e, 1), :]
+        coef[128 * block : 128 * block + 128, :] = jnp.broadcast_to(line, (128, 128)).T
+    gx.forward()
+    gg.direct()
+    gx.diagonal()
+    gx.pair()
+    load_up.wait()
+    gx.finish()
+
+    def cols(n):
+        return pl.ds(pl.multiple_of(n * 256, 256), 256)
+
+    def up_tile(n, carry):
+        pre = dot(x_all[...], up[:, cols(n)], NN)
+        sig = jax.nn.sigmoid(pre)
+        hid[:, cols(n)] = (pre * sig).astype(BF16)
+        slope[:, cols(n)] = sig * (1.0 + pre * (1.0 - sig))
+        return carry
+
+    lax.fori_loop(0, 2, up_tile, 0)
+    gg.forward()
+    lax.fori_loop(2, 4, up_tile, 0)
+    load_down.wait()
+
+    def partial(q, n):
+        if q == 0:
+            scale = coef[...]
+            return dot(hid[...], down[:, cols(n)], NN) * jnp.concatenate([scale, scale], axis=1)
+        return dot(gpre[...], up[cols(n), :], NT)
+
+    def copy_a(q, zz):
+        return remote(send_a.at[q, zz], recv_a.at[q, zz], a_send.at[q, zz], a_recv.at[q, zz], to_sib)
+
+    def copy_b(q, zz, x_first):
+        src = s_sum.at[q, zz, :, xn] if x_first else s_sum.at[q, zz, yn]
+        where = to_x if x_first else to_y
+        return remote(src, recv_1.at[q, zz], b_send.at[q, zz], b_recv.at[q, zz], where)
+
+    def copy_t(q, zz, x_first):
+        where = to_y if x_first else to_x
+        return remote(mid.at[q, zz], recv_2.at[q, zz], t_send.at[q, zz], t_recv.at[q, zz], where)
+
+    def copy_c(q, d):
+        zz, where = at_z(d)
+        return remote(q_sum.at[q, zz], recv_3.at[q, d - 1], c_send.at[q, d - 1], c_recv.at[q, d - 1], where)
+
+    def other_half(q):
+        def body(zz, carry):
+            send_a[q, zz] = partial(q, 2 * zz + 1 - c).astype(BF16)
+            copy_a(q, zz).start()
+            return carry
+        lax.fori_loop(0, 4, body, 0)
+
+    def own_half(q):
+        def body(x_first, zz, carry):
+            part = partial(q, 2 * zz + c)
+            copy_a(q, zz).wait_recv()
+            total = (part + recv_a[q, zz].astype(F32)).astype(BF16)
+            s_sum[q, zz] = total.reshape(2, 2, 128, 256)
+            copy_b(q, zz, x_first).start()
+            return carry
+        lax.fori_loop(0, 2, functools.partial(body, True), 0)
+        lax.fori_loop(2, 4, functools.partial(body, False), 0)
+
+    def second_hop(q):
+        for zz in (0, 2, 1, 3):
+            x_first = zz < 2
+            copy_b(q, zz, x_first).wait_recv()
+            mine = s_sum[q, zz, yn, x] if x_first else s_sum[q, zz, y, xn]
+            got = recv_1[q, zz, yn] if x_first else recv_1[q, zz, xn]
+            mid[q, zz] = (mine.astype(F32) + got.astype(F32)).astype(BF16)
+            copy_t(q, zz, x_first).start()
+
+    def along_z(q):
+        for zz in (0, 2, 1, 3):
+            x_first = zz < 2
+            copy_t(q, zz, x_first).wait_recv()
+            got = recv_1[q, zz, y] if x_first else recv_1[q, zz, x]
+            total = s_sum[q, zz, y, x].astype(F32) + got.astype(F32) + recv_2[q, zz].astype(F32)
+            q_sum[q, zz] = total.astype(BF16)
+        for d in (2, 1, 3):
+            copy_c(q, d).start()
+
+    def result(q, out):
+        total = q_sum[q, z].astype(F32)
+        for d in (1, 2, 3):
+            copy_c(q, d).wait_recv()
+            total = total + recv_3[q, d - 1].astype(F32)
+        out[...] = total.astype(BF16)
+
+    def gup_tile(n, carry):
+        gup[cols(n), :] = dot(x_all[:, cols(n)], gpre[...], TN).astype(BF16)
+        pltpu.make_async_copy(gup.at[cols(n)], gup_hbm.at[cols(n)], gup_sem.at[n]).start()
+        return carry
+
+    def gdown_tile(n, carry):
+        gdown[cols(n), :] = dot(hid[:, cols(n)], gr_all[...], TN).astype(BF16)
+        pltpu.make_async_copy(gdown.at[cols(n)], gdown_hbm.at[cols(n)], gdown_sem.at[n]).start()
+        return carry
+
+    other_half(0)
+    gg.diagonal()
+    gg.pair()
+    own_half(0)
+    gg.finish()
+
+    def scale_tile(n, carry):
+        at = pl.ds(pl.multiple_of(n * 128, 128), 128)
+        gr_all[:, at] = (g_all[:, at].astype(F32) * coef[...]).astype(BF16)
+        return carry
+
+    lax.fori_loop(0, 16, scale_tile, 0)
+
+    def gpre_tile(n, carry):
+        gpre[:, cols(n)] = (dot(gr_all[...], down[cols(n), :], NT) * slope[:, cols(n)]).astype(BF16)
+        return carry
+
+    lax.fori_loop(0, 4, gpre_tile, 0)
+    second_hop(0)
+    other_half(1)
+    own_half(1)
+    along_z(0)
+    lax.fori_loop(0, 4, gdown_tile, 0)
+    second_hop(1)
+    lax.fori_loop(0, 4, gup_tile, 0)
+    along_z(1)
+    lax.fori_loop(4, 8, gup_tile, 0)
+    result(0, mixed_out)
+    result(1, gtok_out)
+
+    gx.drain()
+    gg.drain()
+    for copy in weights:
+        copy.wait_send()
+    for q in (0, 1):
+        for zz in range(4):
+            copy_a(q, zz).wait_send()
+            copy_b(q, zz, zz < 2).wait_send()
+            copy_t(q, zz, zz < 2).wait_send()
+        for d in (1, 2, 3):
+            copy_c(q, d).wait_send()
+    for n in range(8):
+        pltpu.make_async_copy(gup.at[cols(n)], gup_hbm.at[cols(n)], gup_sem.at[n]).wait()
+    for n in range(4):
+        pltpu.make_async_copy(gdown.at[cols(n)], gdown_hbm.at[cols(n)], gdown_sem.at[n]).wait()
+
+
+def fused(tokens, expert_ids, gate_values, grad_out, w_up, w_down):
+    experts = jnp.arange(8, dtype=jnp.int32)[:, None, None]
+    weight = jnp.sum(jnp.where(expert_ids.T[None] == experts, gate_values.T[None], 0.0), axis=1)
+    up, down = w_up[0], w_down[0]
+    width, units = up.shape
+    vmem, dma = pltpu.VMEM, pltpu.SemaphoreType.DMA
+    whole, anywhere = pl.BlockSpec(memory_space=pltpu.VMEM), pl.BlockSpec(memory_space=pl.ANY)
+    small = jax.ShapeDtypeStruct((128, 256), BF16)
+    mixed, gtok, gup, gdown = pl.pallas_call(
+        fused_kernel,
+        out_shape=(
+            small, small,
+            jax.ShapeDtypeStruct((width, units), BF16),
+            jax.ShapeDtypeStruct((units, width), BF16),
+        ),
+        in_specs=[whole] * 3 + [anywhere] * 2,
+        out_specs=(whole, whole, anywhere, anywhere),
+        scratch_shapes=[
+            vmem((512, width), BF16), vmem((512, width), BF16), vmem((512, width), BF16),
+            vmem((4, 8, 128), F32), vmem((512, 128), F32),
+            vmem((width, units), BF16), vmem((units, width), BF16),
+            vmem((512, units), F32), vmem((512, units), BF16), vmem((512, units), BF16),
+            vmem((2, 4, 512, 256), BF16), vmem((2, 4, 512, 256), BF16),
+            vmem((2, 4, 2, 2, 128, 256), BF16), vmem((2, 4, 2, 128, 256), BF16),
+            vmem((2, 4, 128, 256), BF16), vmem((2, 4, 128, 256), BF16),
+            vmem((2, 4, 128, 256), BF16), vmem((2, 3, 128, 256), BF16),
+            vmem((width, units), BF16), vmem((units, width), BF16),
+            dma((2,)), dma((3,)), dma((3,)), dma((2, 13)), dma((2, 13)),
+            dma((2, 4)), dma((2, 4)), dma((2, 4)), dma((2, 4)), dma((2, 4)), dma((2, 4)),
+            dma((2, 3)), dma((2, 3)), dma((8,)), dma((4,)),
+        ],
+        compiler_params=pltpu.CompilerParams(
+            collective_id=0, has_side_effects=True, vmem_limit_bytes=56 * 1024 * 1024
+        ),
+        cost_estimate=pl.CostEstimate(flops=12 * 512 * width * units, bytes_accessed=8 * width * units, transcendentals=512 * units),
+    )(weight, tokens, grad_out, up, down)
+    return mixed, gtok, gup[None], gdown[None]
 
 
 def plan_slots(routed, experts, capacity):
@@ -49,6 +361,8 @@
 def local(tokens, expert_ids, gate_values, grad_out, w_up, w_down):
     n_rep = lax.axis_size("rep")
     n_exp = lax.axis_size("exp")
+    if (n_rep, n_exp) == (8, 4) and tokens.shape == (128, 2048) and w_up.shape[2] == 1024:
+        return fused(tokens, expert_ids, gate_values, grad_out, w_up, w_down)
     tok_count, width = tokens.shape
     top_k = expert_ids.shape[1]
     pair_count = tok_count * top_k

time: 218 us -> 75.6 us (0.35)
  waiting for transfers between devices: 129 us -> 0 us
  Pallas kernels: 0 us -> 63.6 us
  matrix products: 38.5 us -> 0 us
  starting transfers between devices: 21.4 us -> 0 us
  between operations: 14.2 us -> 0.64 us
  other arithmetic: 5.69 us -> 1.29 us
    psum x1 -> x0, waiting for transfers between devices: 97.3 us -> none  [local(): lax.psum(out_part.astype(jnp.bfloat16), 'rep').astype(jnp.float32)]
    pallas_call x0 -> x1, Pallas kernels: none -> 63.6 us  [fused(): pl.pallas_call(fused_kernel, out_shape=(small, small, jax.ShapeDtypeStruc...]
    dot_general x10 -> x0, matrix products: 38.5 us -> none  [the longest x1 6.25 us: expert_math(): lax.dot_general(rows_in, gradient_before_activation, (((0,), (0,)), ((),...]
    all_to_all x5 -> x0, waiting for transfers between devices: 31.5 us -> none  [the longest x1 16.2 us: local(): lax.all_to_all(sent_in.reshape(n_exp, capacity, width), 'exp', split_axis...]
    all_to_all x5 -> x0, starting transfers between devices: 21.4 us -> none  [the longest x1 5.16 us: local(): lax.all_to_all(count_parts, 'exp', split_axis=0, concat_axis=0, tiled=True)]
    unnamed x16 -> x6, local copies, waits for them, and re-layouts: 3.36 us -> 9.78 us
    mul x3 -> x0, local copies, waits for them, and re-layouts: 3.62 us -> none  [local(): gate_values[:, :, None] * grad_out[:, None, :].astype(jnp.float32)]
    convert_element_type x3 -> x0, other arithmetic: 3.35 us -> none  [the longest x1 1.69 us: local(): summed_dx.astype(jnp.bfloat16).reshape(n_exp, capacity, cols)]
  transfers between devices with their start and end apart: 6 -> 0, of which waited for: 4 -> 0; matrix products, arithmetic and copies ran while one was open for 16% -> 0% of each run, Pallas kernels for 0% -> 0%
where the time goes in v1:
time: 75.6 us; the launch traced here: 75.4 us
  Pallas kernels  63.6 us (84%)
  local copies, waits for them, and re-layouts  9.78 us (13%)
  other arithmetic  1.29 us (2%)
    pallas_call x1, Pallas kernels, fused(): pl.pallas_call(fused_kernel, out_shape=(small, small, jax.ShapeDtypeStruc...  63.6 us
    unnamed x6, local copies, waits for them, and re-layouts  9.78 us

profile of v1, /device:TPU:0, one launch (start us, length us, event | category | flops | bytes accessed | tf_op | source)
XLA Modules:
  0.0 75.4 jit_solution(13807213093612149888)
XLA Ops:
  0.6 1.3 %select_reduce_fusion.weight_in = f32[8,128]{1,0:T(8,128)} fusion(f32[2,128]{1,0:T(2,128)} %bitcast.8, s32[2,128]{1,0:T(2,128)} %bitcast.9), kind=kLoop, calls=%fused_computation | loop fusion | flops 5120 | bytes 6144 | tf_op jit(solution)/shard_map/reduce_sum | solution.py:282
  1.9 63.6 %shard_map.93 = (bf16[128,256]{1,0:T(8,128)(2,1)}, bf16[128,256]{1,0:T(8,128)(2,1)}, bf16[2048,1024]{1,0:T(8,128)(2,1)}, bf16[1024,2048]{1,0:T(8,128)(2,1)}) custom-call(f32[8,128]{1,0:T(8,128)} %select_reduce_fusion.weight_in, bf16[128,2048]{1,0:T(8,128)(2,1)} %tok.1, bf16[128,2048]{1,0:T(8,128)(2,1)} %gout.1, bf16[2048,1024]{1,0:T(8,128)(2,1)} %bitcast.10, ...), custom_call_target="tpu_custom_call" | custom-call | flops 12884901888 | bytes 16777216 | tf_op jit(solution)/shard_map/pallas_call | solution.py:288
  65.6 1.5 %copy.14 = bf16[128,256]{1,0:T(8,128)(2,1)} copy(bf16[128,256]{1,0:T(8,128)(2,1)} %get-tuple-element.16) | data formatting | bytes 131072
  67.1 1.5 %copy.15 = bf16[128,256]{1,0:T(8,128)(2,1)} copy(bf16[128,256]{1,0:T(8,128)(2,1)} %get-tuple-element.17) | data formatting | bytes 131072
  68.5 0.0 copy-start
  68.5 4.8 %copy.16 = bf16[1,2048,1024]{2,1,0:T(8,128)(2,1)} copy(bf16[1,2048,1024]{2,1,0:T(8,128)(2,1)} %bitcast.7) | data formatting | bytes 8388608
  73.3 0.0 copy-done
  73.3 2.0 %copy.17 = bf16[1,1024,2048]{2,1,0:T(8,128)(2,1)} copy(bf16[1,1024,2048]{2,1,0:T(8,128)(2,1)S(1)} %bitcast.6) | data formatting | bytes 8388608
Async XLA Ops:
  68.5 4.8 %copy-start = (bf16[1024,2048]{1,0:T(8,128)(2,1)S(1)}, bf16[1024,2048]{1,0:T(8,128)(2,1)}, u32[]{:S(2)}) copy-start(bf16[1024,2048]{1,0:T(8,128)(2,1)} %get-tuple-element.11) | copy-start | bytes 12582916

commit v2 on v1

--- a/solution.py
+++ b/solution.py
@@ -20,7 +20,7 @@
 
 
 def fused_kernel(
-    weight_in, tok, gout, up_hbm, down_hbm,
+    ids, gates, tok, gout, up_hbm, down_hbm,
     mixed_out, gtok_out, gup_hbm, gdown_hbm,
     x_all, g_all, gr_all, weight_all, coef, up, down, slope, hid, gpre,
     send_a, recv_a, s_sum, recv_1, mid, recv_2, q_sum, recv_3, gup, gdown,
@@ -79,144 +79,170 @@
             self.copies[k] = copy
 
         def direct(self):
-            mine = self.own.at[pl.ds(pl.multiple_of(lo, 16), 48)]
-            self.send(0, mine, e, lo, 48, to_x)
-            self.send(1, mine, e, lo, 48, to_y)
+            own_piece, mid_piece = (own_rows, 16), (mid_rows, 32)
+            self.pieces = (own_piece, mid_piece) if self.t == 0 else (mid_piece, own_piece)
+            first, second = self.pieces
+            for k, (start, count), where in ((0, first, to_x), (1, second, to_y), (2, second, to_x), (3, first, to_y)):
+                mine = self.own.at[pl.ds(pl.multiple_of(start, 16), count)]
+                self.send(k, mine, e, start, count, where)
 
         def keep(self):
             self.buf[rows(e, 0, 128), :] = self.own[...]
 
-        def forward(self):
-            first = (own_rows, 16) if self.t == 0 else (mid_rows, 32)
-            second = (mid_rows, 32) if self.t == 0 else (own_rows, 16)
+        def around(self):
+            first, second = self.pieces
             self.copies[0].wait_recv()
-            self.send(2, None, ex, *first, to_y)
-            self.send(4, None, ex, own_rows, 16, to_pair)
-            self.send(7, None, ex, lo, 48, to_sib)
+            self.send(4, None, ex, *first, to_y)
             self.copies[1].wait_recv()
-            self.send(3, None, ey, *second, to_x)
-            self.send(5, None, ey, own_rows, 16, to_pair)
-            self.send(8, None, ey, lo, 48, to_sib)
+            self.send(5, None, ey, *second, to_x)
+
+        def share(self):
+            self.copies[2].wait_recv()
+            self.send(6, None, ex, own_rows, 16, to_pair)
+            self.send(9, None, ex, lo, 48, to_sib)
+            self.copies[3].wait_recv()
+            self.send(7, None, ey, own_rows, 16, to_pair)
+            self.send(10, None, ey, lo, 48, to_sib)
 
         def diagonal(self):
-            self.copies[2].wait_recv()
-            self.copies[3].wait_recv()
-            self.send(6, None, ed, own_rows, 16, to_pair)
-            self.send(9, None, ed, lo, 48, to_sib)
+            self.copies[4].wait_recv()
+            self.copies[5].wait_recv()
+            self.send(8, None, ed, own_rows, 16, to_pair)
+            self.send(11, None, ed, lo, 48, to_sib)
 
         def pair(self):
-            for k, block in ((4, ex), (5, ey), (6, ed)):
+            for k, block in ((6, ex), (7, ey), (8, ed)):
                 self.copies[k].wait_recv()
                 self.send(6 + k, None, block, pair_rows, 16, to_sib)
 
-        def finish(self):
-            for k in range(7, 13):
-                self.copies[k].wait_recv()
+        def finish(self, blocks):
+            for k in blocks:
+                self.copies[9 + k].wait_recv()
+                self.copies[12 + k].wait_recv()
 
         def drain(self):
-            for k in range(13):
+            for k in range(15):
                 self.copies[k].wait_send()
 
     gx, gg = Gather(0, tok, x_all), Gather(1, gout, g_all)
     gx.direct()
+    expert = lax.broadcasted_iota(jnp.int32, (8, 128), 0)
+    first_gate = jnp.where(ids[0:1, :] == expert, gates[0:1, :], 0.0)
+    weight_all[pl.ds(e, 1)] = (first_gate + jnp.where(ids[1:2, :] == expert, gates[1:2, :], 0.0))[None]
     weights = []
     for k, where in enumerate((to_x, to_y, to_d)):
-        copy = remote(weight_in, weight_all.at[e], meta_send.at[k], meta_recv.at[k], where)
+        copy = remote(weight_all.at[e], weight_all.at[e], meta_send.at[k], meta_recv.at[k], where)
         copy.start()
         weights.append(copy)
     gx.keep()
     gg.keep()
-    weight_all[pl.ds(e, 1)] = weight_in[...][None]
+    gx.around()
+    gg.direct()
+    gx.share()
     for copy in weights:
         copy.wait_recv()
     for block in range(4):
         line = weight_all[block, pl.ds(e, 1), :]
         coef[128 * block : 128 * block + 128, :] = jnp.broadcast_to(line, (128, 128)).T
-    gx.forward()
-    gg.direct()
     gx.diagonal()
     gx.pair()
     load_up.wait()
-    gx.finish()
 
     def cols(n):
         return pl.ds(pl.multiple_of(n * 256, 256), 256)
 
-    def up_tile(n, carry):
-        pre = dot(x_all[...], up[:, cols(n)], NN)
-        sig = jax.nn.sigmoid(pre)
-        hid[:, cols(n)] = (pre * sig).astype(BF16)
-        slope[:, cols(n)] = sig * (1.0 + pre * (1.0 - sig))
-        return carry
-
-    lax.fori_loop(0, 2, up_tile, 0)
-    gg.forward()
-    lax.fori_loop(2, 4, up_tile, 0)
+    def up_half(yy):
+        for n in range(4):
+            pre = dot(x_all[cols(yy), :], up[:, cols(n)], NN)
+            sig = jax.nn.sigmoid(pre)
+            hid[cols(yy), cols(n)] = (pre * sig).astype(BF16)
+            slope[cols(yy), cols(n)] = sig * (1.0 + pre * (1.0 - sig))
+
+    gx.finish((0,))
+    up_half(y)
+    gg.around()
+    gx.finish((1, 2))
+    up_half(yn)
+    gg.share()
     load_down.wait()
 
-    def partial(q, n):
+    def partial(q, yy, n):
         if q == 0:
-            scale = coef[...]
-            return dot(hid[...], down[:, cols(n)], NN) * jnp.concatenate([scale, scale], axis=1)
-        return dot(gpre[...], up[cols(n), :], NT)
-
-    def copy_a(q, zz):
-        return remote(send_a.at[q, zz], recv_a.at[q, zz], a_send.at[q, zz], a_recv.at[q, zz], to_sib)
-
-    def copy_b(q, zz, x_first):
-        src = s_sum.at[q, zz, :, xn] if x_first else s_sum.at[q, zz, yn]
-        where = to_x if x_first else to_y
-        return remote(src, recv_1.at[q, zz], b_send.at[q, zz], b_recv.at[q, zz], where)
-
-    def copy_t(q, zz, x_first):
-        where = to_y if x_first else to_x
+            scale = coef[cols(yy), :]
+            return dot(hid[cols(yy), :], down[:, cols(n)], NN) * jnp.concatenate([scale, scale], axis=1)
+        return dot(gpre[cols(yy), :], up[cols(n), :], NT)
+
+    def copy_a(q, yy, zz):
+        return remote(
+            send_a.at[q, zz, yy], recv_a.at[q, zz, yy], a_send.at[q, zz, yy], a_recv.at[q, zz, yy], to_sib
+        )
+
+    def copy_bx(q, yy, zz):
+        return remote(
+            s_sum.at[q, zz, yy, xn], recv_1.at[q, zz, yy], b_send.at[q, zz, yy], b_recv.at[q, zz, yy], to_x
+        )
+
+    def copy_by(q, zz):
+        return remote(s_sum.at[q, zz, yn], recv_1.at[q, zz], b_send.at[q, zz, 0], b_recv.at[q, zz, 0], to_y)
+
+    def copy_t(q, zz):
+        where = to_y if zz < 2 else to_x
         return remote(mid.at[q, zz], recv_2.at[q, zz], t_send.at[q, zz], t_recv.at[q, zz], where)
 
-    def copy_c(q, d):
-        zz, where = at_z(d)
+    def copy_c(q, zz, d):
+        where = {"rep": zz * 2 + c, "exp": e}
         return remote(q_sum.at[q, zz], recv_3.at[q, d - 1], c_send.at[q, d - 1], c_recv.at[q, d - 1], where)
 
-    def other_half(q):
+    def other_half(q, yy):
         def body(zz, carry):
-            send_a[q, zz] = partial(q, 2 * zz + 1 - c).astype(BF16)
-            copy_a(q, zz).start()
+            send_a[q, zz, yy] = partial(q, yy, 2 * zz + 1 - c).astype(BF16)
+            copy_a(q, yy, zz).start()
             return carry
         lax.fori_loop(0, 4, body, 0)
 
-    def own_half(q):
+    def own_half(q, yy, far):
         def body(x_first, zz, carry):
-            part = partial(q, 2 * zz + c)
-            copy_a(q, zz).wait_recv()
-            total = (part + recv_a[q, zz].astype(F32)).astype(BF16)
-            s_sum[q, zz] = total.reshape(2, 2, 128, 256)
-            copy_b(q, zz, x_first).start()
+            part = partial(q, yy, 2 * zz + c)
+            copy_a(q, yy, zz).wait_recv()
+            total = (part + recv_a[q, zz, yy].astype(F32)).astype(BF16)
+            s_sum[q, zz, yy] = total.reshape(2, 128, 256)
+            if x_first:
+                copy_bx(q, yy, zz).start()
+            elif far:
+                copy_by(q, zz).start()
             return carry
+        lax.fori_loop(2, 4, functools.partial(body, False), 0)
         lax.fori_loop(0, 2, functools.partial(body, True), 0)
-        lax.fori_loop(2, 4, functools.partial(body, False), 0)
-
-    def second_hop(q):
-        for zz in (0, 2, 1, 3):
-            x_first = zz < 2
-            copy_b(q, zz, x_first).wait_recv()
-            mine = s_sum[q, zz, yn, x] if x_first else s_sum[q, zz, y, xn]
-            got = recv_1[q, zz, yn] if x_first else recv_1[q, zz, xn]
+
+    def second_hop(q, zs):
+        for zz in zs:
+            if zz < 2:
+                copy_bx(q, yn, zz).wait_recv()
+                mine, got = s_sum[q, zz, yn, x], recv_1[q, zz, yn]
+            else:
+                copy_by(q, zz).wait_recv()
+                mine, got = s_sum[q, zz, y, xn], recv_1[q, zz, xn]
             mid[q, zz] = (mine.astype(F32) + got.astype(F32)).astype(BF16)
-            copy_t(q, zz, x_first).start()
-
-    def along_z(q):
-        for zz in (0, 2, 1, 3):
-            x_first = zz < 2
-            copy_t(q, zz, x_first).wait_recv()
-            got = recv_1[q, zz, y] if x_first else recv_1[q, zz, x]
+            copy_t(q, zz).start()
+
+    def along_z(q, zs):
+        for zz in zs:
+            if zz < 2:
+                copy_bx(q, y, zz).wait_recv()
+            copy_t(q, zz).wait_recv()
+            got = recv_1[q, zz, y] if zz < 2 else recv_1[q, zz, x]
             total = s_sum[q, zz, y, x].astype(F32) + got.astype(F32) + recv_2[q, zz].astype(F32)
             q_sum[q, zz] = total.astype(BF16)
-        for d in (2, 1, 3):
-            copy_c(q, d).start()
+            d = lax.rem(zz - z + 4, 4)
+
+            @pl.when(d > 0)
+            def _():
+                copy_c(q, zz, d).start()
 
     def result(q, out):
         total = q_sum[q, z].astype(F32)
         for d in (1, 2, 3):
-            copy_c(q, d).wait_recv()
+            copy_c(q, lax.rem(z + d, 4), d).wait_recv()
             total = total + recv_3[q, d - 1].astype(F32)
         out[...] = total.astype(BF16)
 
@@ -230,33 +256,42 @@
         pltpu.make_async_copy(gdown.at[cols(n)], gdown_hbm.at[cols(n)], gdown_sem.at[n]).start()
         return carry
 
-    other_half(0)
+    other_half(0, y)
     gg.diagonal()
+    own_half(0, y, False)
+    other_half(0, yn)
     gg.pair()
-    own_half(0)
-    gg.finish()
-
-    def scale_tile(n, carry):
-        at = pl.ds(pl.multiple_of(n * 128, 128), 128)
-        gr_all[:, at] = (g_all[:, at].astype(F32) * coef[...]).astype(BF16)
-        return carry
-
-    lax.fori_loop(0, 16, scale_tile, 0)
-
-    def gpre_tile(n, carry):
-        gpre[:, cols(n)] = (dot(gr_all[...], down[cols(n), :], NT) * slope[:, cols(n)]).astype(BF16)
-        return carry
-
-    lax.fori_loop(0, 4, gpre_tile, 0)
-    second_hop(0)
-    other_half(1)
-    own_half(1)
-    along_z(0)
+    own_half(0, yn, True)
+    gg.finish((0, 1, 2))
+
+    def scale_half(yy):
+        for n in range(16):
+            at = pl.ds(n * 128, 128)
+            gr_all[cols(yy), at] = (g_all[cols(yy), at].astype(F32) * coef[cols(yy), :]).astype(BF16)
+
+    def gpre_half(yy):
+        for n in range(4):
+            grad = dot(gr_all[cols(yy), :], down[cols(n), :], NT)
+            gpre[cols(yy), cols(n)] = (grad * slope[cols(yy), cols(n)]).astype(BF16)
+
+    order = (2, 0, 3, 1)
+    scale_half(yn)
+    gpre_half(yn)
+    second_hop(0, order)
+    other_half(1, yn)
+    own_half(1, yn, True)
+    scale_half(y)
+    gpre_half(y)
+    along_z(0, order)
+    other_half(1, y)
+    second_hop(1, (0, 1))
+    own_half(1, y, False)
+    second_hop(1, (2, 3))
     lax.fori_loop(0, 4, gdown_tile, 0)
-    second_hop(1)
-    lax.fori_loop(0, 4, gup_tile, 0)
-    along_z(1)
-    lax.fori_loop(4, 8, gup_tile, 0)
+    along_z(1, (0, 2))
+    lax.fori_loop(0, 1, gup_tile, 0)
+    along_z(1, (1, 3))
+    lax.fori_loop(1, 8, gup_tile, 0)
     result(0, mixed_out)
     result(1, gtok_out)
 
@@ -266,53 +301,77 @@
         copy.wait_send()
     for q in (0, 1):
         for zz in range(4):
-            copy_a(q, zz).wait_send()
-            copy_b(q, zz, zz < 2).wait_send()
-            copy_t(q, zz, zz < 2).wait_send()
+            for yy in (0, 1):
+                copy_a(q, yy, zz).wait_send()
+            if zz < 2:
+                copy_bx(q, 0, zz).wait_send()
+                copy_bx(q, 1, zz).wait_send()
+            else:
+                copy_by(q, zz).wait_send()
+            copy_t(q, zz).wait_send()
         for d in (1, 2, 3):
-            copy_c(q, d).wait_send()
+            copy_c(q, lax.rem(z + d, 4), d).wait_send()
     for n in range(8):
         pltpu.make_async_copy(gup.at[cols(n)], gup_hbm.at[cols(n)], gup_sem.at[n]).wait()
     for n in range(4):
         pltpu.make_async_copy(gdown.at[cols(n)], gdown_hbm.at[cols(n)], gdown_sem.at[n]).wait()
 
 
+def settle_kernel(mixed, gtok, gup, gdown, mixed_out, gtok_out, gup_out, gdown_out, sem):
+    pieces = [(mixed, mixed_out), (gtok, gtok_out)]
+    for src, dst in ((gup, gup_out), (gdown, gdown_out)):
+        step = src.shape[0] // 8
+        pieces += [(src.at[pl.ds(k * step, step)], dst.at[pl.ds(k * step, step)]) for k in range(8)]
+    copies = [pltpu.make_async_copy(src, dst, sem.at[k]) for k, (src, dst) in enumerate(pieces)]
+    for copy in copies:
+        copy.start()
+    for copy in copies:
+        copy.wait()
+
+
 def fused(tokens, expert_ids, gate_values, grad_out, w_up, w_down):
-    experts = jnp.arange(8, dtype=jnp.int32)[:, None, None]
-    weight = jnp.sum(jnp.where(expert_ids.T[None] == experts, gate_values.T[None], 0.0), axis=1)
     up, down = w_up[0], w_down[0]
     width, units = up.shape
     vmem, dma = pltpu.VMEM, pltpu.SemaphoreType.DMA
     whole, anywhere = pl.BlockSpec(memory_space=pltpu.VMEM), pl.BlockSpec(memory_space=pl.ANY)
     small = jax.ShapeDtypeStruct((128, 256), BF16)
-    mixed, gtok, gup, gdown = pl.pallas_call(
+    shapes = (
+        small, small,
+        jax.ShapeDtypeStruct((width, units), BF16),
+        jax.ShapeDtypeStruct((units, width), BF16),
+    )
+    found = pl.pallas_call(
         fused_kernel,
-        out_shape=(
-            small, small,
-            jax.ShapeDtypeStruct((width, units), BF16),
-            jax.ShapeDtypeStruct((units, width), BF16),
-        ),
-        in_specs=[whole] * 3 + [anywhere] * 2,
+        out_shape=shapes,
+        in_specs=[whole] * 4 + [anywhere] * 2,
         out_specs=(whole, whole, anywhere, anywhere),
         scratch_shapes=[
             vmem((512, width), BF16), vmem((512, width), BF16), vmem((512, width), BF16),
             vmem((4, 8, 128), F32), vmem((512, 128), F32),
             vmem((width, units), BF16), vmem((units, width), BF16),
             vmem((512, units), F32), vmem((512, units), BF16), vmem((512, units), BF16),
-            vmem((2, 4, 512, 256), BF16), vmem((2, 4, 512, 256), BF16),
+            vmem((2, 4, 2, 256, 256), BF16), vmem((2, 4, 2, 256, 256), BF16),
             vmem((2, 4, 2, 2, 128, 256), BF16), vmem((2, 4, 2, 128, 256), BF16),
             vmem((2, 4, 128, 256), BF16), vmem((2, 4, 128, 256), BF16),
             vmem((2, 4, 128, 256), BF16), vmem((2, 3, 128, 256), BF16),
             vmem((width, units), BF16), vmem((units, width), BF16),
-            dma((2,)), dma((3,)), dma((3,)), dma((2, 13)), dma((2, 13)),
-            dma((2, 4)), dma((2, 4)), dma((2, 4)), dma((2, 4)), dma((2, 4)), dma((2, 4)),
+            dma((2,)), dma((3,)), dma((3,)), dma((2, 15)), dma((2, 15)),
+            dma((2, 4, 2)), dma((2, 4, 2)), dma((2, 4, 2)), dma((2, 4, 2)), dma((2, 4)), dma((2, 4)),
             dma((2, 3)), dma((2, 3)), dma((8,)), dma((4,)),
         ],
         compiler_params=pltpu.CompilerParams(
             collective_id=0, has_side_effects=True, vmem_limit_bytes=56 * 1024 * 1024
         ),
         cost_estimate=pl.CostEstimate(flops=12 * 512 * width * units, bytes_accessed=8 * width * units, transcendentals=512 * units),
-    )(weight, tokens, grad_out, up, down)
+    )(expert_ids.T, gate_values.T, tokens, grad_out, up, down)
+    mixed, gtok, gup, gdown = pl.pallas_call(
+        settle_kernel,
+        out_shape=shapes,
+        in_specs=[anywhere] * 4,
+        out_specs=(anywhere,) * 4,
+        scratch_shapes=[dma((18,))],
+        compiler_params=pltpu.CompilerParams(vmem_limit_bytes=60 * 1024 * 1024),
+    )(*found)
     return mixed, gtok, gup[None], gdown[None]
 
 

time: 75.6 us -> 321 us (4.25)
  Pallas kernels: 63.6 us -> 320 us
  local copies, waits for them, and re-layouts: 9.78 us -> 0 us
    pallas_call x1 -> x2, Pallas kernels: 63.6 us -> 320 us  [the longest x1 259 us: fused(): pl.pallas_call(settle_kernel, out_shape=shapes, in_specs=[anywhere] * 4,...]
    unnamed x6 -> x0, local copies, waits for them, and re-layouts: 9.78 us -> none
where the time goes in v2:
time: 321 us
  Pallas kernels  320 us (100%)
    pallas_call x1, Pallas kernels, fused(): pl.pallas_call(settle_kernel, out_shape=shapes, in_specs=[anywhere] * 4,...  259 us
    pallas_call x1, Pallas kernels, fused(): pl.pallas_call(fused_kernel, out_shape=shapes, in_specs=[whole] * 4 + [an...  60.7 us

profile of v2, /device:TPU:0, one launch (start us, length us, event | category | flops | bytes accessed | tf_op | source)
XLA Modules:
  0.0 320.7 jit_solution(12496461495613483483)
XLA Ops:
  0.6 60.7 %shard_map.93 = (bf16[128,256]{1,0:T(8,128)(2,1)}, bf16[128,256]{1,0:T(8,128)(2,1)}, bf16[2048,1024]{1,0:T(8,128)(2,1)}, bf16[1024,2048]{1,0:T(8,128)(2,1)}) custom-call(s32[2,128]{1,0:T(2,128)} %bitcast.10, f32[2,128]{1,0:T(2,128)} %bitcast.11, bf16[128,2048]{1,0:T(8,128)(2,1)} %tok.1, bf16[128,2048]{1,0:T(8,128)(2,1)} %gout.1, bf16[2048,1024]{1,0:T(8,128)(2,1)} %bitcast.6, ...), custom_call_target="tpu_custom_call" | custom-call | flops 12884901888 | bytes 16777216 | tf_op jit(solution)/shard_map/pallas_call | solution.py:343
  61.3 259.3 %shard_map.94 = (bf16[128,256]{1,0:T(8,128)(2,1)}, bf16[128,256]{1,0:T(8,128)(2,1)}, bf16[2048,1024]{1,0:T(8,128)(2,1)}, bf16[1024,2048]{1,0:T(8,128)(2,1)}) custom-call(bf16[128,256]{1,0:T(8,128)(2,1)} %get-tuple-element.12.mixed, bf16[128,256]{1,0:T(8,128)(2,1)} %get-tuple-element.13.gtok, bf16[2048,1024]{1,0:T(8,128)(2,1)} %get-tuple-element.14.gup, ...), custom_call_target="tpu_custom_call" | custom-call | tf_op jit(solution)/shard_map/pallas_call | solution.py:367

commit v3 on v2

--- a/solution.py
+++ b/solution.py
@@ -21,11 +21,11 @@
 
 def fused_kernel(
     ids, gates, tok, gout, up_hbm, down_hbm,
-    mixed_out, gtok_out, gup_hbm, gdown_hbm,
+    mixed_out, gtok_out, gup, gdown,
     x_all, g_all, gr_all, weight_all, coef, up, down, slope, hid, gpre,
-    send_a, recv_a, s_sum, recv_1, mid, recv_2, q_sum, recv_3, gup, gdown,
+    send_a, recv_a, s_sum, recv_1, mid, recv_2, q_sum, recv_3,
     load_sem, meta_send, meta_recv, gat_send, gat_recv,
-    a_send, a_recv, b_send, b_recv, t_send, t_recv, c_send, c_recv, gup_sem, gdown_sem,
+    a_send, a_recv, b_send, b_recv, t_send, t_recv, c_send, c_recv,
 ):
     rep, e = lax.axis_index("rep"), lax.axis_index("exp")
     z, c = lax.div(rep, 2), lax.rem(rep, 2)
@@ -110,10 +110,10 @@
             self.send(8, None, ed, own_rows, 16, to_pair)
             self.send(11, None, ed, lo, 48, to_sib)
 
-        def pair(self):
-            for k, block in ((6, ex), (7, ey), (8, ed)):
-                self.copies[k].wait_recv()
-                self.send(6 + k, None, block, pair_rows, 16, to_sib)
+        def pair(self, blocks=(0, 1, 2)):
+            for k in blocks:
+                self.copies[6 + k].wait_recv()
+                self.send(12 + k, None, (ex, ey, ed)[k], pair_rows, 16, to_sib)
 
         def finish(self, blocks):
             for k in blocks:
@@ -144,33 +144,36 @@
     for block in range(4):
         line = weight_all[block, pl.ds(e, 1), :]
         coef[128 * block : 128 * block + 128, :] = jnp.broadcast_to(line, (128, 128)).T
-    gx.diagonal()
-    gx.pair()
     load_up.wait()
 
     def cols(n):
         return pl.ds(pl.multiple_of(n * 256, 256), 256)
 
-    def up_half(yy):
-        for n in range(4):
+    def up_tiles(yy, tiles):
+        for n in tiles:
             pre = dot(x_all[cols(yy), :], up[:, cols(n)], NN)
             sig = jax.nn.sigmoid(pre)
             hid[cols(yy), cols(n)] = (pre * sig).astype(BF16)
             slope[cols(yy), cols(n)] = sig * (1.0 + pre * (1.0 - sig))
 
+    gx.pair((0, 1))
     gx.finish((0,))
-    up_half(y)
+    up_tiles(y, (0, 1))
+    gx.diagonal()
     gg.around()
+    up_tiles(y, (2, 3))
+    gx.pair((2,))
+    gg.share()
     gx.finish((1, 2))
-    up_half(yn)
-    gg.share()
+    up_tiles(yn, (0, 1, 2, 3))
     load_down.wait()
 
     def partial(q, yy, n):
+        at = slice(None) if yy is None else cols(yy)
         if q == 0:
-            scale = coef[cols(yy), :]
-            return dot(hid[cols(yy), :], down[:, cols(n)], NN) * jnp.concatenate([scale, scale], axis=1)
-        return dot(gpre[cols(yy), :], up[cols(n), :], NT)
+            scale = coef[at, :]
+            return dot(hid[at, :], down[:, cols(n)], NN) * jnp.concatenate([scale, scale], axis=1)
+        return dot(gpre[at, :], up[cols(n), :], NT)
 
     def copy_a(q, yy, zz):
         return remote(
@@ -194,25 +197,38 @@
         return remote(q_sum.at[q, zz], recv_3.at[q, d - 1], c_send.at[q, d - 1], c_recv.at[q, d - 1], where)
 
     def other_half(q, yy):
-        def body(zz, carry):
-            send_a[q, zz, yy] = partial(q, yy, 2 * zz + 1 - c).astype(BF16)
-            copy_a(q, yy, zz).start()
-            return carry
-        lax.fori_loop(0, 4, body, 0)
+        halves = (0, 1) if yy is None else (yy,)
+        for pair in ((2, 3), (0, 1)):
+            for zz in pair:
+                part = partial(q, yy, 2 * zz + 1 - c).astype(BF16)
+                if yy is None:
+                    send_a[q, zz] = part.reshape(2, 256, 256)
+                else:
+                    send_a[q, zz, yy] = part
+            for zz in pair:
+                for half in halves:
+                    copy_a(q, half, zz).start()
 
     def own_half(q, yy, far):
-        def body(x_first, zz, carry):
-            part = partial(q, yy, 2 * zz + c)
-            copy_a(q, yy, zz).wait_recv()
-            total = (part + recv_a[q, zz, yy].astype(F32)).astype(BF16)
-            s_sum[q, zz, yy] = total.reshape(2, 128, 256)
-            if x_first:
-                copy_bx(q, yy, zz).start()
-            elif far:
-                copy_by(q, zz).start()
-            return carry
-        lax.fori_loop(2, 4, functools.partial(body, False), 0)
-        lax.fori_loop(0, 2, functools.partial(body, True), 0)
+        halves = (0, 1) if yy is None else (yy,)
+        for pair in ((2, 3), (0, 1)):
+            for zz in pair:
+                for half in halves:
+                    copy_a(q, half, zz).wait_recv()
+            for zz in pair:
+                part = partial(q, yy, 2 * zz + c)
+                if yy is None:
+                    total = part + recv_a[q, zz].reshape(512, 256).astype(F32)
+                    s_sum[q, zz] = total.astype(BF16).reshape(2, 2, 128, 256)
+                else:
+                    total = part + recv_a[q, zz, yy].astype(F32)
+                    s_sum[q, zz, yy] = total.astype(BF16).reshape(2, 128, 256)
+            for zz in pair:
+                if zz < 2:
+                    for half in halves:
+                        copy_bx(q, half, zz).start()
+                elif far:
+                    copy_by(q, zz).start()
 
     def second_hop(q, zs):
         for zz in zs:
@@ -248,20 +264,16 @@
 
     def gup_tile(n, carry):
         gup[cols(n), :] = dot(x_all[:, cols(n)], gpre[...], TN).astype(BF16)
-        pltpu.make_async_copy(gup.at[cols(n)], gup_hbm.at[cols(n)], gup_sem.at[n]).start()
         return carry
 
     def gdown_tile(n, carry):
         gdown[cols(n), :] = dot(hid[:, cols(n)], gr_all[...], TN).astype(BF16)
-        pltpu.make_async_copy(gdown.at[cols(n)], gdown_hbm.at[cols(n)], gdown_sem.at[n]).start()
         return carry
 
-    other_half(0, y)
+    other_half(0, None)
     gg.diagonal()
-    own_half(0, y, False)
-    other_half(0, yn)
     gg.pair()
-    own_half(0, yn, True)
+    own_half(0, None, True)
     gg.finish((0, 1, 2))
 
     def scale_half(yy):
@@ -287,11 +299,11 @@
     second_hop(1, (0, 1))
     own_half(1, y, False)
     second_hop(1, (2, 3))
-    lax.fori_loop(0, 4, gdown_tile, 0)
+    lax.fori_loop(0, 4, gdown_tile, 0, unroll=2)
     along_z(1, (0, 2))
-    lax.fori_loop(0, 1, gup_tile, 0)
+    lax.fori_loop(0, 2, gup_tile, 0, unroll=2)
     along_z(1, (1, 3))
-    lax.fori_loop(1, 8, gup_tile, 0)
+    lax.fori_loop(2, 8, gup_tile, 0, unroll=2)
     result(0, mixed_out)
     result(1, gtok_out)
 
@@ -311,20 +323,18 @@
             copy_t(q, zz).wait_send()
         for d in (1, 2, 3):
             copy_c(q, lax.rem(z + d, 4), d).wait_send()
-    for n in range(8):
-        pltpu.make_async_copy(gup.at[cols(n)], gup_hbm.at[cols(n)], gup_sem.at[n]).wait()
-    for n in range(4):
-        pltpu.make_async_copy(gdown.at[cols(n)], gdown_hbm.at[cols(n)], gdown_sem.at[n]).wait()
 
 
 def settle_kernel(mixed, gtok, gup, gdown, mixed_out, gtok_out, gup_out, gdown_out, sem):
-    pieces = [(mixed, mixed_out), (gtok, gtok_out)]
+    pieces = []
     for src, dst in ((gup, gup_out), (gdown, gdown_out)):
         step = src.shape[0] // 8
         pieces += [(src.at[pl.ds(k * step, step)], dst.at[pl.ds(k * step, step)]) for k in range(8)]
     copies = [pltpu.make_async_copy(src, dst, sem.at[k]) for k, (src, dst) in enumerate(pieces)]
     for copy in copies:
         copy.start()
+    mixed_out[...] = mixed[...]
+    gtok_out[...] = gtok[...]
     for copy in copies:
         copy.wait()
 
@@ -342,9 +352,9 @@
     )
     found = pl.pallas_call(
         fused_kernel,
-        out_shape=shapes,
+        out_shape=(small, small, pltpu.VMEM((width, units), BF16), pltpu.VMEM((units, width), BF16)),
         in_specs=[whole] * 4 + [anywhere] * 2,
-        out_specs=(whole, whole, anywhere, anywhere),
+        out_specs=(whole,) * 4,
         scratch_shapes=[
             vmem((512, width), BF16), vmem((512, width), BF16), vmem((512, width), BF16),
             vmem((4, 8, 128), F32), vmem((512, 128), F32),
@@ -354,23 +364,22 @@
             vmem((2, 4, 2, 2, 128, 256), BF16), vmem((2, 4, 2, 128, 256), BF16),
             vmem((2, 4, 128, 256), BF16), vmem((2, 4, 128, 256), BF16),
             vmem((2, 4, 128, 256), BF16), vmem((2, 3, 128, 256), BF16),
-            vmem((width, units), BF16), vmem((units, width), BF16),
             dma((2,)), dma((3,)), dma((3,)), dma((2, 15)), dma((2, 15)),
             dma((2, 4, 2)), dma((2, 4, 2)), dma((2, 4, 2)), dma((2, 4, 2)), dma((2, 4)), dma((2, 4)),
-            dma((2, 3)), dma((2, 3)), dma((8,)), dma((4,)),
+            dma((2, 3)), dma((2, 3)),
         ],
         compiler_params=pltpu.CompilerParams(
-            collective_id=0, has_side_effects=True, vmem_limit_bytes=56 * 1024 * 1024
+            collective_id=0, has_side_effects=True, vmem_limit_bytes=44 * 1024 * 1024
         ),
         cost_estimate=pl.CostEstimate(flops=12 * 512 * width * units, bytes_accessed=8 * width * units, transcendentals=512 * units),
     )(expert_ids.T, gate_values.T, tokens, grad_out, up, down)
     mixed, gtok, gup, gdown = pl.pallas_call(
         settle_kernel,
         out_shape=shapes,
-        in_specs=[anywhere] * 4,
-        out_specs=(anywhere,) * 4,
-        scratch_shapes=[dma((18,))],
-        compiler_params=pltpu.CompilerParams(vmem_limit_bytes=60 * 1024 * 1024),
+        in_specs=[whole, whole, whole, whole],
+        out_specs=(whole, whole, anywhere, anywhere),
+        scratch_shapes=[dma((16,))],
+        compiler_params=pltpu.CompilerParams(vmem_limit_bytes=16 * 1024 * 1024),
     )(*found)
     return mixed, gtok, gup[None], gdown[None]
 

time: 321 us -> 66.8 us (0.21)
  Pallas kernels: 320 us -> 61.7 us
  local copies, waits for them, and re-layouts: 0 us -> 3.43 us
    pallas_call x2, Pallas kernels: 320 us -> 61.7 us  [the longest x1 57.6 us: fused(): pl.pallas_call(fused_kernel, out_shape=(small, small, pltpu.VMEM((width,...]
    unnamed x0 -> x8, local copies, waits for them, and re-layouts: none -> 3.43 us
where the time goes in v3:
time: 66.8 us; the launch traced here: 65.9 us
  Pallas kernels  61.7 us (92%)
  local copies, waits for them, and re-layouts  3.43 us (5%)
  between operations  0.81 us (1%)
    pallas_call x1, Pallas kernels, fused(): pl.pallas_call(fused_kernel, out_shape=(small, small, pltpu.VMEM((width,...  57.6 us
    pallas_call x1, Pallas kernels, fused(): pl.pallas_call(settle_kernel, out_shape=shapes, in_specs=[whole, whole, w...  4.07 us
    unnamed x8, local copies, waits for them, and re-layouts  3.43 us

profile of v3, /device:TPU:0, one launch (start us, length us, event | category | flops | bytes accessed | tf_op | source)
XLA Modules:
  0.0 65.9 jit_solution(8631180677151952130)
XLA Ops:
  0.6 0.0 copy-start
  0.6 1.0 %copy-done = bf16[128,2048]{1,0:T(8,128)(2,1)S(1)} copy-done((bf16[128,2048]{1,0:T(8,128)(2,1)S(1)}, bf16[128,2048]{1,0:T(8,128)(2,1)}, u32[]{:S(2)}) %copy-start) | copy-done | bytes 524312
  1.7 0.0 copy-start.1
  1.7 1.0 %copy-done.1 = bf16[128,2048]{1,0:T(8,128)(2,1)S(1)} copy-done((bf16[128,2048]{1,0:T(8,128)(2,1)S(1)}, bf16[128,2048]{1,0:T(8,128)(2,1)}, u32[]{:S(2)}) %copy-start.1) | copy-done | bytes 524312
  2.7 0.0 copy-start.2
  2.7 0.7 %copy-done.2 = s32[128,2]{0,1:T(2,128)S(1)} copy-done((s32[128,2]{0,1:T(2,128)S(1)}, s32[128,2]{0,1:T(2,128)}, u32[]{:S(2)}) %copy-start.2) | copy-done | bytes 1048
  3.4 0.0 copy-start.3
  3.4 0.7 %copy-done.3 = f32[128,2]{0,1:T(2,128)S(1)} copy-done((f32[128,2]{0,1:T(2,128)S(1)}, f32[128,2]{0,1:T(2,128)}, u32[]{:S(2)}) %copy-start.3) | copy-done | bytes 1048
  4.1 57.6 %shard_map.93 = (bf16[128,256]{1,0:T(8,128)(2,1)S(1)}, bf16[128,256]{1,0:T(8,128)(2,1)S(1)}, bf16[2048,1024]{1,0:T(8,128)(2,1)S(1)}, bf16[1024,2048]{1,0:T(8,128)(2,1)S(1)}) custom-call(s32[2,128]{1,0:T(2,128)S(1)} %bitcast.6, f32[2,128]{1,0:T(2,128)S(1)} %bitcast.7, bf16[128,2048]{1,0:T(8,128)(2,1)S(1)} %copy-done, bf16[128,2048]{1,0:T(8,128)(2,1)S(1)} %copy-done.1, ...), custom_call_target="tpu_custom_call" | custom-call | flops 12884901888 | bytes 16777216 | tf_op jit(solution)/shard_map/pallas_call | solution.py:353
  61.7 4.1 %shard_map.94 = (bf16[128,256]{1,0:T(8,128)(2,1)}, bf16[128,256]{1,0:T(8,128)(2,1)}, bf16[2048,1024]{1,0:T(8,128)(2,1)}, bf16[1024,2048]{1,0:T(8,128)(2,1)}) custom-call(bf16[128,256]{1,0:T(8,128)(2,1)S(1)} %get-tuple-element.12.mixed, bf16[128,256]{1,0:T(8,128)(2,1)S(1)} %get-tuple-element.13.gtok, bf16[2048,1024]{1,0:T(8,128)(2,1)S(1)} %get-tuple-element.14.gup, ...), custom_call_target="tpu_custom_call" | custom-call | tf_op jit(solution)/shard_map/pallas_call | solution.py:376
Async XLA Ops:
  0.6 1.0 %copy-start = (bf16[128,2048]{1,0:T(8,128)(2,1)S(1)}, bf16[128,2048]{1,0:T(8,128)(2,1)}, u32[]{:S(2)}) copy-start(bf16[128,2048]{1,0:T(8,128)(2,1)} %tok.1) | copy-start | bytes 1572868
  1.7 1.0 %copy-start.1 = (bf16[128,2048]{1,0:T(8,128)(2,1)S(1)}, bf16[128,2048]{1,0:T(8,128)(2,1)}, u32[]{:S(2)}) copy-start(bf16[128,2048]{1,0:T(8,128)(2,1)} %gout.1) | copy-start | bytes 1572868
  2.7 0.7 %copy-start.2 = (s32[128,2]{0,1:T(2,128)S(1)}, s32[128,2]{0,1:T(2,128)}, u32[]{:S(2)}) copy-start(s32[128,2]{0,1:T(2,128)} %param.7) | copy-start | bytes 3076
  3.4 0.7 %copy-start.3 = (f32[128,2]{0,1:T(2,128)S(1)}, f32[128,2]{0,1:T(2,128)}, u32[]{:S(2)}) copy-start(f32[128,2]{0,1:T(2,128)} %param.8) | copy-start | bytes 3076

commit v4 on v3

--- a/solution.py
+++ b/solution.py
@@ -20,9 +20,9 @@
 
 
 def fused_kernel(
-    ids, gates, tok, gout, up_hbm, down_hbm,
-    mixed_out, gtok_out, gup, gdown,
-    x_all, g_all, gr_all, weight_all, coef, up, down, slope, hid, gpre,
+    ids_hbm, gates_hbm, tok, gout, up_hbm, down_hbm,
+    mixed_out, gtok_out, x_all, gpre, gdown,
+    ids, gates, g_all, gr_all, weight_all, coef, up, down, slope, hid,
     send_a, recv_a, s_sum, recv_1, mid, recv_2, q_sum, recv_3,
     load_sem, meta_send, meta_recv, gat_send, gat_recv,
     a_send, a_recv, b_send, b_recv, t_send, t_recv, c_send, c_recv,
@@ -51,8 +51,10 @@
 
     load_up = pltpu.make_async_copy(up_hbm, up, load_sem.at[0])
     load_down = pltpu.make_async_copy(down_hbm, down, load_sem.at[1])
-    load_up.start()
-    load_down.start()
+    load_ids = pltpu.make_async_copy(ids_hbm, ids, load_sem.at[2])
+    load_gates = pltpu.make_async_copy(gates_hbm, gates, load_sem.at[3])
+    load_ids.start()
+    load_gates.start()
 
     barrier = pltpu.get_barrier_semaphore()
     partners = [to_x, to_y, to_d, to_sib] + [at_z(d)[1] for d in (1, 2, 3)]
@@ -87,27 +89,31 @@
                 self.send(k, mine, e, start, count, where)
 
         def keep(self):
-            self.buf[rows(e, 0, 128), :] = self.own[...]
+            self.own_copy = pltpu.make_async_copy(self.own, self.buf.at[rows(e, 0, 128)], load_sem.at[4 + self.t])
+            self.own_copy.start()
 
         def around(self):
             first, second = self.pieces
             self.copies[0].wait_recv()
             self.send(4, None, ex, *first, to_y)
+            if self.t == 0:
+                self.send(6, None, ex, own_rows, 16, to_pair)
             self.copies[1].wait_recv()
             self.send(5, None, ey, *second, to_x)
 
         def share(self):
             self.copies[2].wait_recv()
-            self.send(6, None, ex, own_rows, 16, to_pair)
+            if self.t == 1:
+                self.send(6, None, ex, own_rows, 16, to_pair)
             self.send(9, None, ex, lo, 48, to_sib)
             self.copies[3].wait_recv()
             self.send(7, None, ey, own_rows, 16, to_pair)
             self.send(10, None, ey, lo, 48, to_sib)
 
         def diagonal(self):
-            self.copies[4].wait_recv()
-            self.copies[5].wait_recv()
+            self.copies[4 + self.t].wait_recv()
             self.send(8, None, ed, own_rows, 16, to_pair)
+            self.copies[5 - self.t].wait_recv()
             self.send(11, None, ed, lo, 48, to_sib)
 
         def pair(self, blocks=(0, 1, 2)):
@@ -126,6 +132,12 @@
 
     gx, gg = Gather(0, tok, x_all), Gather(1, gout, g_all)
     gx.direct()
+    gx.keep()
+    load_up.start()
+    gg.keep()
+    load_down.start()
+    load_ids.wait()
+    load_gates.wait()
     expert = lax.broadcasted_iota(jnp.int32, (8, 128), 0)
     first_gate = jnp.where(ids[0:1, :] == expert, gates[0:1, :], 0.0)
     weight_all[pl.ds(e, 1)] = (first_gate + jnp.where(ids[1:2, :] == expert, gates[1:2, :], 0.0))[None]
@@ -134,8 +146,6 @@
         copy = remote(weight_all.at[e], weight_all.at[e], meta_send.at[k], meta_recv.at[k], where)
         copy.start()
         weights.append(copy)
-    gx.keep()
-    gg.keep()
     gx.around()
     gg.direct()
     gx.share()
@@ -157,6 +167,7 @@
             slope[cols(yy), cols(n)] = sig * (1.0 + pre * (1.0 - sig))
 
     gx.pair((0, 1))
+    gx.own_copy.wait()
     gx.finish((0,))
     up_tiles(y, (0, 1))
     gx.diagonal()
@@ -262,10 +273,6 @@
             total = total + recv_3[q, d - 1].astype(F32)
         out[...] = total.astype(BF16)
 
-    def gup_tile(n, carry):
-        gup[cols(n), :] = dot(x_all[:, cols(n)], gpre[...], TN).astype(BF16)
-        return carry
-
     def gdown_tile(n, carry):
         gdown[cols(n), :] = dot(hid[:, cols(n)], gr_all[...], TN).astype(BF16)
         return carry
@@ -274,6 +281,7 @@
     gg.diagonal()
     gg.pair()
     own_half(0, None, True)
+    gg.own_copy.wait()
     gg.finish((0, 1, 2))
 
     def scale_half(yy):
@@ -299,11 +307,10 @@
     second_hop(1, (0, 1))
     own_half(1, y, False)
     second_hop(1, (2, 3))
-    lax.fori_loop(0, 4, gdown_tile, 0, unroll=2)
+    lax.fori_loop(0, 2, gdown_tile, 0, unroll=2)
     along_z(1, (0, 2))
-    lax.fori_loop(0, 2, gup_tile, 0, unroll=2)
+    lax.fori_loop(2, 4, gdown_tile, 0, unroll=2)
     along_z(1, (1, 3))
-    lax.fori_loop(2, 8, gup_tile, 0, unroll=2)
     result(0, mixed_out)
     result(1, gtok_out)
 
@@ -325,16 +332,21 @@
             copy_c(q, lax.rem(z + d, 4), d).wait_send()
 
 
-def settle_kernel(mixed, gtok, gup, gdown, mixed_out, gtok_out, gup_out, gdown_out, sem):
-    pieces = []
-    for src, dst in ((gup, gup_out), (gdown, gdown_out)):
-        step = src.shape[0] // 8
-        pieces += [(src.at[pl.ds(k * step, step)], dst.at[pl.ds(k * step, step)]) for k in range(8)]
-    copies = [pltpu.make_async_copy(src, dst, sem.at[k]) for k, (src, dst) in enumerate(pieces)]
-    for copy in copies:
-        copy.start()
+def settle_kernel(mixed, gtok, x_all, gpre, gdown, mixed_out, gtok_out, gup_out, gdown_out, gup, sem):
+    copies = []
+    step = gdown.shape[0] // 4
+    for k in range(4):
+        at = pl.ds(k * step, step)
+        copies.append(pltpu.make_async_copy(gdown.at[at], gdown_out.at[at], sem.at[k]))
+        copies[-1].start()
     mixed_out[...] = mixed[...]
     gtok_out[...] = gtok[...]
+    step = gup.shape[0] // 8
+    for k in range(8):
+        at = pl.ds(k * step, step)
+        gup[at, :] = dot(x_all[:, at], gpre[...], TN).astype(BF16)
+        copies.append(pltpu.make_async_copy(gup.at[at], gup_out.at[at], sem.at[4 + k]))
+        copies[-1].start()
     for copy in copies:
         copy.wait()
 
@@ -352,19 +364,23 @@
     )
     found = pl.pallas_call(
         fused_kernel,
-        out_shape=(small, small, pltpu.VMEM((width, units), BF16), pltpu.VMEM((units, width), BF16)),
-        in_specs=[whole] * 4 + [anywhere] * 2,
-        out_specs=(whole,) * 4,
+        out_shape=(
+            small, small, pltpu.VMEM((512, width), BF16), pltpu.VMEM((512, units), BF16),
+            pltpu.VMEM((units, width), BF16),
+        ),
+        in_specs=[pl.BlockSpec(memory_space=pltpu.HBM)] * 4 + [anywhere] * 2,
+        out_specs=(whole,) * 5,
         scratch_shapes=[
-            vmem((512, width), BF16), vmem((512, width), BF16), vmem((512, width), BF16),
+            vmem((2, 128), jnp.int32), vmem((2, 128), F32),
+            vmem((512, width), BF16), vmem((512, width), BF16),
             vmem((4, 8, 128), F32), vmem((512, 128), F32),
             vmem((width, units), BF16), vmem((units, width), BF16),
-            vmem((512, units), F32), vmem((512, units), BF16), vmem((512, units), BF16),
+            vmem((512, units), F32), vmem((512, units), BF16),
             vmem((2, 4, 2, 256, 256), BF16), vmem((2, 4, 2, 256, 256), BF16),
             vmem((2, 4, 2, 2, 128, 256), BF16), vmem((2, 4, 2, 128, 256), BF16),
             vmem((2, 4, 128, 256), BF16), vmem((2, 4, 128, 256), BF16),
             vmem((2, 4, 128, 256), BF16), vmem((2, 3, 128, 256), BF16),
-            dma((2,)), dma((3,)), dma((3,)), dma((2, 15)), dma((2, 15)),
+            dma((6,)), dma((3,)), dma((3,)), dma((2, 15)), dma((2, 15)),
             dma((2, 4, 2)), dma((2, 4, 2)), dma((2, 4, 2)), dma((2, 4, 2)), dma((2, 4)), dma((2, 4)),
             dma((2, 3)), dma((2, 3)),
         ],
@@ -372,14 +388,14 @@
             collective_id=0, has_side_effects=True, vmem_limit_bytes=44 * 1024 * 1024
         ),
         cost_estimate=pl.CostEstimate(flops=12 * 512 * width * units, bytes_accessed=8 * width * units, transcendentals=512 * units),
-    )(expert_ids.T, gate_values.T, tokens, grad_out, up, down)
+    )(*(pltpu.with_memory_space_constraint(a, pltpu.HBM) for a in (expert_ids.T, gate_values.T, tokens, grad_out)), up, down)
     mixed, gtok, gup, gdown = pl.pallas_call(
         settle_kernel,
         out_shape=shapes,
-        in_specs=[whole, whole, whole, whole],
+        in_specs=[whole] * 5,
         out_specs=(whole, whole, anywhere, anywhere),
-        scratch_shapes=[dma((16,))],
-        compiler_params=pltpu.CompilerParams(vmem_limit_bytes=16 * 1024 * 1024),
+        scratch_shapes=[pltpu.VMEM((width, units), BF16), dma((12,))],
+        compiler_params=pltpu.CompilerParams(vmem_limit_bytes=24 * 1024 * 1024),
     )(*found)
     return mixed, gtok, gup[None], gdown[None]
 

time: 66.8 us -> 62.5 us (0.936)
  local copies, waits for them, and re-layouts: 3.43 us -> 0 us
    unnamed x8 -> x0, local copies, waits for them, and re-layouts: 3.43 us -> none
where the time goes in v4:
time: 62.5 us; the launch traced here: 61.9 us
  Pallas kernels  61.2 us (98%)
  between operations  0.64 us (1%)
    pallas_call x1, Pallas kernels, fused(): pl.pallas_call(fused_kernel, out_shape=(small, small, pltpu.VMEM((512, wi...  57.2 us
    pallas_call x1, Pallas kernels, fused(): pl.pallas_call(settle_kernel, out_shape=shapes, in_specs=[whole] * 5, out...  4.08 us

profile of v4, /device:TPU:0, one launch (start us, length us, event | category | flops | bytes accessed | tf_op | source)
XLA Modules:
  0.0 61.9 jit_solution(15795401749078317966)
XLA Ops:
  0.6 57.2 %shard_map.93 = (bf16[128,256]{1,0:T(8,128)(2,1)S(1)}, bf16[128,256]{1,0:T(8,128)(2,1)S(1)}, bf16[512,2048]{1,0:T(8,128)(2,1)S(1)}, bf16[512,1024]{1,0:T(8,128)(2,1)S(1)}, bf16[1024,2048]{1,0:T(8,128)(2,1)S(1)}) custom-call(s32[2,128]{1,0:T(2,128)} %bitcast.10, f32[2,128]{1,0:T(2,128)} %bitcast.11, bf16[128,2048]{1,0:T(8,128)(2,1)} %tok.1, ...), custom_call_target="tpu_custom_call" | custom-call | flops 12884901888 | bytes 16777216 | tf_op jit(solution)/shard_map/pallas_call | solution.py:365
  57.8 4.1 %shard_map.94 = (bf16[128,256]{1,0:T(8,128)(2,1)}, bf16[128,256]{1,0:T(8,128)(2,1)}, bf16[2048,1024]{1,0:T(8,128)(2,1)}, bf16[1024,2048]{1,0:T(8,128)(2,1)}) custom-call(bf16[128,256]{1,0:T(8,128)(2,1)S(1)} %get-tuple-element.13.mixed, bf16[128,256]{1,0:T(8,128)(2,1)S(1)} %get-tuple-element.14.gtok, bf16[512,2048]{1,0:T(8,128)(2,1)S(1)} %get-tuple-element.15.x_all, ...), custom_call_target="tpu_custom_call" | custom-call | tf_op jit(solution)/shard_map/pallas_call | solution.py:392
